TPU v7x, 128 devices: a whole 4x4x4 slice. The times are simulated.
128 devices in a mesh: grp: 4 (over x), mem: 32 (over y, z, core).
Axes of the slice: x: 4, y: 4, z: 4, core: 2. Of those that a mesh axis runs over, the one named last changes fastest.
Arguments:
- vectors: float32 [131072, 768], P(('grp', 'mem')), may hold values from -6 to 6
- boundary: float32 [8192, 768], P(('grp', 'mem')), may hold values from -6 to 6
- centroids: float32 [32768, 768], P(('grp', 'mem')), may hold values from -3 to 3
- list_owner: int32 [8192, 8], P(('grp', 'mem')), may hold values from 0 to 127, all different within a row; in each aligned block of 64 rows (0 to 63, 64 to 127, ...) at most 8 rows name the same one
- list_slot: int32 [8192, 8], P(('grp', 'mem')), may hold values from 0 to 255
Outputs:
- resident_score: bfloat16 [131072, 8192], P(('grp', 'mem'))
- posting_residual: float32 [131072, 768], P(('grp', 'mem'))
- posting_dist: float32 [128, 1024], P(('grp', 'mem'))
Inputs may be any that keep to these rules, and one draw needn't show every extreme that they name: `list_owner`: A row names 8 different owners. Among the rows of one device no owner is named by more than 8 rows, a bound that some block reaches.
All inputs are finite; a program needn't handle non-finite values.
Results may differ from a plain program's by a relative error of at most 0.006.
Values may be sent and summed in bfloat16 or wider, within the bound.
A program may use at most 192 MiB of HBM per device.

v0:
```python
import math

import jax
import jax.numpy as jnp
from jax import lax
from jax.sharding import PartitionSpec as P

D = 768
LIST = 8
BROWS = 64


def on_device(vectors, boundary, centroids, list_owner, list_slot):
    group_count = lax.axis_size("grp")
    member_count = lax.axis_size("mem")
    devices = group_count * member_count
    capacity = 16 * BROWS // devices
    factor = 1.0 / math.sqrt(D)
    vec_bf = vectors.astype(jnp.bfloat16)
    cen_bf = centroids.astype(jnp.bfloat16)
    cen_norm = jnp.sum(centroids * centroids, axis=1)
    contract = (((1,), (1,)), ((), ()))
    panel_rows = lax.all_gather(cen_bf, "mem", axis=0, tiled=True)
    panel_norms = lax.all_gather(cen_norm, "mem", axis=0, tiled=True)
    products = lax.dot_general(vec_bf, panel_rows, contract, preferred_element_type=jnp.float32)
    scores = ((2.0 * products - panel_norms[None, :]) * factor).astype(jnp.bfloat16)
    owners = list_owner.reshape(-1)
    slot_list = list_slot.reshape(-1)
    onehot = (owners[:, None] == jnp.arange(devices, dtype=jnp.int32)[None, :]).astype(jnp.int32)
    before = jnp.cumsum(onehot, axis=0) - onehot
    places = jnp.sum(before * onehot, axis=1)
    target = owners * capacity + places
    sent_rows = jnp.repeat(boundary, LIST, axis=0)
    vec_buffer = jnp.zeros((devices * capacity, D), jnp.float32).at[target].set(sent_rows)
    slot_buffer = (
        jnp.full((devices * capacity,), -1.0, jnp.float32)
        .at[target]
        .set(slot_list.astype(jnp.float32))
    )
    arrived = lax.all_to_all(
        vec_buffer.reshape(devices, capacity, D).astype(jnp.bfloat16),
        ("grp", "mem"),
        split_axis=0,
        concat_axis=0,
        tiled=True,
    ).astype(jnp.float32)
    slot_value = lax.all_to_all(
        slot_buffer.reshape(devices, capacity).astype(jnp.bfloat16),
        ("grp", "mem"),
        split_axis=0,
        concat_axis=0,
        tiled=True,
    ).astype(jnp.float32)
    slot_index = slot_value.astype(jnp.int32)
    filled = slot_index >= 0
    centre = centroids[jnp.maximum(slot_index, 0)]
    residual = jnp.where(filled[..., None], arrived - centre, 0.0)
    residual, distance = (residual, jnp.sum(residual * residual, axis=-1) / D)
    return (
        scores,
        residual.reshape(devices * capacity, D),
        distance.reshape(1, devices * capacity),
    )


def solution(mesh):
    return jax.shard_map(
        on_device,
        mesh=mesh,
        in_specs=(
            P(("grp", "mem"), None),
            P(("grp", "mem"), None),
            P(("grp", "mem"), None),
            P(("grp", "mem"), None),
            P(("grp", "mem"), None),
        ),
        out_specs=(P(("grp", "mem"), None), P(("grp", "mem"), None), P(("grp", "mem"), None)),
        check_vma=False,
    )
```

profile of v0, /device:TPU:1, one launch (start us, length us, event | category | flops | bytes accessed | tf_op | source)
XLA Modules:
  0.0 122.7 jit_solution(5963846240980714942)
XLA Ops:
  7.2 0.0 copy-start
  7.2 0.0 all-gather.3.cloned.1.call-start
  7.2 2.3 %multiply_reduce_fusion.1 = (f32[256]{0:T(256)S(1)}, bf16[256,768]{1,0:T(8,128)(2,1)}) fusion(f32[256,768]{1,0:T(8,128)} %param.7), kind=kLoop, calls=%fused_computation.14 | loop fusion | flops 589568 | bytes 1180672 | tf_op jit(solution)/shard_map/reduce_sum | solution.py:21
  9.6 0.0 all-gather.3.cloned.1.call-update
  9.6 0.8 copy.22
  10.4 0.1 eq.29
  10.5 0.1 eq.25
  10.6 0.7 broadcast_multiply_fusion.1
  11.3 0.1 copy.21
  11.3 0.1 mul.44
  11.4 0.1 copy.24
  11.5 0.2 fusion.9
  11.9 0.1 copy.26
  12.0 0.1 reshape.133
  12.1 0.2 fusion.8
  12.3 2.4 %scatter_custom_fusion = f32[1024]{0:T(1024)S(1)} fusion(s32[512]{0:T(512)S(1)} %bitcast.43, f32[512]{0:T(512)S(1)} %reshape.133, f32[]{:T(128)} %constant.11.clone.1), kind=kCustom, calls=%fused_computation.32 | custom fusion | bytes 4100 | tf_op jit(solution)/shard_map/scatter | solution.py:38
  14.8 0.7 convert_element_type.88
  15.5 11.5 %all-to-all-start = ((bf16[128,1,8]{2,1,0:T(2,128)(2,1)}), bf16[128,1,8]{2,1,0:T(2,128)(2,1)S(1)}, u32[]{:S(2)}, u32[]{:S(2)}) async-start(bf16[128,1,8]{2,1,0:T(2,128)(2,1)} %convert_element_type.88), calls=%async_computation | async-start | bytes 131072 | tf_op jit(solution)/shard_map/all_to_all | solution.py:47
  27.0 4.2 %scatter_custom_fusion.1 = f32[1024,768]{1,0:T(8,128)} fusion(s32[512]{0:T(512)S(1)} %bitcast.44, f32[]{:T(128)} %constant.9.clone.1, f32[64,768]{1,0:T(8,128)S(1)} %copy-done), kind=kCustom, calls=%fused_computation.8 | custom fusion | bytes 3342340 | tf_op jit(solution)/shard_map/scatter | solution.py:34
  31.2 3.3 %convert_bitcast_fusion = bf16[128,8,768]{2,1,0:T(8,128)(2,1)} fusion(f32[1024,768]{1,0:T(8,128)} %scatter_custom_fusion.1), kind=kLoop, calls=%fused_computation.10 | loop fusion | flops 786432 | bytes 4718592 | tf_op jit(solution)/shard_map/convert_element_type | solution.py:41
  34.5 1.9 %all-to-all-done = bf16[128,1,8]{2,1,0:T(2,128)(2,1)S(1)} async-done(((bf16[128,1,8]{2,1,0:T(2,128)(2,1)}), bf16[128,1,8]{2,1,0:T(2,128)(2,1)S(1)}, u32[]{:S(2)}, u32[]{:S(2)}) %all-to-all-start) | async-done | bytes 2080 | tf_op jit(solution)/shard_map/all_to_all | solution.py:47
  36.4 7.9 %all-to-all-start.1 = ((bf16[128,8,768]{2,1,0:T(8,128)(2,1)}), bf16[128,8,768]{2,1,0:T(8,128)(2,1)S(1)}, u32[]{:S(2)}, u32[]{:S(2)}) async-start(bf16[128,8,768]{2,1,0:T(8,128)(2,1)} %convert_bitcast_fusion), calls=%async_computation.1 | async-start | bytes 3145728 | tf_op jit(solution)/shard_map/all_to_all | solution.py:40
  44.3 41.2 %all-gather = f32[32,1,256]{2,1,0:T(1,128)S(1)} all-gather(f32[1,1,256]{2,1,0:T(1,128)S(1)} %bitcast.42), channel_id=1, replica_groups=mesh['grp'=4,'mem'=32] {'mem'}, dimensions={0}, use_global_device_ids=true | all-gather | bytes 33792 | tf_op jit(solution)/shard_map/all_gather | solution.py:24
  85.5 0.1 copy.28
  85.6 0.1 copy.30
  85.7 0.1 reshape.123
  85.8 5.2 %gather_fusion = f32[1024,768]{1,0:T(8,128)} fusion(f32[256,768]{1,0:T(8,128)S(1)} %copy-done.1, s32[1024]{0:T(1024)S(1)} %broadcast_clamp_fusion), kind=kCustom, calls=%fused_computation | custom fusion | bytes 6295552 | tf_op jit(solution)/shard_map/gather | solution.py:56
  91.1 0.1 copy.29
  91.2 0.0 all-to-all-done.1
  91.2 4.3 %multiply_reduce_fusion = (f32[128,8]{1,0:T(8,128)S(1)}, f32[1024,768]{1,0:T(8,128)}) fusion(f32[1024,768]{1,0:T(8,128)} %gather_fusion, bf16[128,8,768]{2,1,0:T(8,128)(2,1)S(1)} %all-to-all-done.1, pred[128,8]{1,0:T(8,128)(4,1)S(1)} %copy.29), kind=kLoop, calls=%fused_computation.6 | loop fusion | flops 3931136 | bytes 7869440 | tf_op jit(solution)/shard_map/reduce_sum | solution.py:58
  95.5 0.7 div.10
  96.2 19.7 %multiply_convert_fusion = bf16[1024,8192]{1,0:T(8,128)(2,1)} fusion(bf16[8192,768]{1,0:T(8,128)(2,1)} %all-gather.3.cloned.1.call-done, f32[8192]{0:T(1024)S(1)} %bitcast.39, f32[1024,768]{1,0:T(8,128)} %param.5), kind=kOutput, calls=%fused_computation.3 | convolution fusion | flops 12919242752 | bytes 32538624 | tf_op jit(solution)/shard_map/dot_general | solution.py:25
  (19 shorter events, 0.1 us)
Async XLA Ops:
  7.2 19.9 %copy-start = (f32[64,768]{1,0:T(8,128)S(1)}, f32[64,768]{1,0:T(8,128)}, u32[]{:S(2)}) copy-start(f32[64,768]{1,0:T(8,128)} %param.6) | copy-start | bytes 589828
  7.2 4.7 %copy-start.2 = (s32[64,8]{0,1:T(8,128)S(1)}, s32[64,8]{0,1:T(8,128)}, u32[]{:S(2)}) copy-start(s32[64,8]{0,1:T(8,128)} %param.9) | copy-start | bytes 6148
  7.2 89.0 %all-gather.3.cloned.1.call-start = ((), (), s32[]{:S(2)}) async-start(), calls=%async_computation.2 | async-start | bytes 12976128 | tf_op jit(solution)/shard_map/all_gather | solution.py:23
  15.5 20.9 %all-to-all-start = ((bf16[128,1,8]{2,1,0:T(2,128)(2,1)}), bf16[128,1,8]{2,1,0:T(2,128)(2,1)S(1)}, u32[]{:S(2)}, u32[]{:S(2)}) async-start(bf16[128,1,8]{2,1,0:T(2,128)(2,1)} %convert_element_type.88), calls=%async_computation | async-start | bytes 131072 | tf_op jit(solution)/shard_map/all_to_all | solution.py:47
  31.2 54.6 %copy-start.1 = (f32[256,768]{1,0:T(8,128)S(1)}, f32[256,768]{1,0:T(8,128)}, u32[]{:S(2)}) copy-start(f32[256,768]{1,0:T(8,128)} %param.7) | copy-start | bytes 2359300
  36.4 54.8 %all-to-all-start.1 = ((bf16[128,8,768]{2,1,0:T(8,128)(2,1)}), bf16[128,8,768]{2,1,0:T(8,128)(2,1)S(1)}, u32[]{:S(2)}, u32[]{:S(2)}) async-start(bf16[128,8,768]{2,1,0:T(8,128)(2,1)} %convert_bitcast_fusion), calls=%async_computation.1 | async-start | bytes 3145728 | tf_op jit(solution)/shard_map/all_to_all | solution.py:40
Sparse Core Ops, SparseCore 0:
  10.3 82.4 all-gather.2
where the time goes:
time: 123 us
  blocking collectives  41.2 us (33%)
  matrix products  19.7 us (16%)
  starting transfers between devices  19.5 us (16%)
  local copies, waits for them, and re-layouts  15.1 us (12%)
  between operations  14.2 us (12%)
  other arithmetic  11.1 us (9%)
  waiting for transfers between devices  1.94 us (2%)
    all_gather x1, blocking collectives, on_device(): panel_norms = lax.all_gather(cen_norm, 'mem', axis=0, tiled=True)  41.2 us
    dot_general x1, matrix products, on_device(): lax.dot_general(vec_bf, panel_rows, contract, preferred_element_type=jnp....  19.7 us
    all_to_all x1, starting transfers between devices, on_device(): lax.all_to_all(slot_buffer.reshape(devices, capacity).astype(jnp.bfloat16...  11.5 us
    all_to_all x1, starting transfers between devices, on_device(): lax.all_to_all(vec_buffer.reshape(devices, capacity, D).astype(jnp.bfloat...  7.92 us
    gather x1, local copies, waits for them, and re-layouts, on_device(): centre = centroids[jnp.maximum(slot_index, 0)]  5.23 us
    reduce_sum x1, other arithmetic, on_device(): residual, distance = (residual, jnp.sum(residual * residual, axis=-1) / D)  4.26 us
    scatter x1, local copies, waits for them, and re-layouts, on_device(): jnp.zeros((devices * capacity, D), jnp.float32).at[target].set(sent_rows)  4.17 us
    convert_element_type x1, other arithmetic, on_device(): vec_buffer.reshape(devices, capacity, D).astype(jnp.bfloat16)  3.26 us
  transfers between devices with their start and end apart: 3, of which 1 were waited for; matrix products, arithmetic and copies ran while one was open for 19% of the time, Pallas kernels for 0%

commit v1 on v0

v1 whole, which is shorter than its diff:
```python
import functools
import math

import jax
import jax.numpy as jnp
from jax import lax
from jax.experimental import pallas as pl
from jax.experimental.pallas import tpu as pltpu
from jax.sharding import PartitionSpec as P

D = 768
LIST = 8
CAP = 8
BROWS = 64
CEN = 256
V_DEV = 1024
N_GRP = 4
N_MEM = 32
RING = 4
CHIPS = 16
DEVICES = 128
WIDE = D + 128
FIELD = 512
MESH = pl.DeviceIdType.MESH
FACTOR = 1.0 / math.sqrt(D)
LATER = 4
LAG = 2

ORDER = (
    (0, 0), (3, 0), (1, 0), (0, 3), (0, 1), (2, 0), (3, 3), (3, 1),
    (1, 3), (1, 1), (0, 2), (2, 3), (2, 1), (3, 2), (1, 2), (2, 2),
)
PLACE = {offset: e for e, offset in enumerate(ORDER)}


def sends_of(e):
    da, db = ORDER[e]
    out = []
    if db == 0:
        if da == 0:
            out += [("a", 1, None, PLACE[3, 0]), ("a", 3, None, PLACE[1, 0])]
        elif da == 3:
            out += [("a", 1, 0, PLACE[2, 0])]
        elif da == 1:
            out += [("a", 3, 1, PLACE[2, 0])]
        out += [("b", 1, None, PLACE[da, 3]), ("b", 3, None, PLACE[da, 1])]
    elif db == 3:
        out += [("b", 1, 0, PLACE[da, 2])]
    elif db == 1:
        out += [("b", 3, 1, PLACE[da, 2])]
    return out + [("core", 0, None, e)]


SENDS = [sends_of(e) for e in range(CHIPS)]
FIRST = [sum(len(s) for s in SENDS[:e]) for e in range(CHIPS)]
N_SENDS = sum(len(s) for s in SENDS)


def split(order):
    da, db = ORDER[order]
    return db == 2 or (db == 0 and da == 2)


def position():
    m = lax.axis_index("mem")
    return lax.axis_index("grp"), m // 8, (m // 2) % RING, m % 2


def member(y, z, core, da, db):
    dy = (1 - core) * da + core * db
    dz = (1 - core) * db + core * da
    return (((y + dy) % RING) * RING + (z + dz) % RING) * 2 + core


def offsets(e):
    da = sum(jnp.where(e == k, o[0], 0) for k, o in enumerate(ORDER))
    db = sum(jnp.where(e == k, o[1], 0) for k, o in enumerate(ORDER))
    return da, db


class Stream:
    def __init__(self, buffer, halves, send, recv, recv_core, where):
        self.buffer, self.halves = buffer, halves
        self.send, self.recv, self.recv_core = send, recv, recv_core
        self.x, self.y, self.z, self.core = where

    def block(self, e, half):
        da, db = ORDER[e]
        ref = self.buffer.at[member(self.y, self.z, self.core, da, db)]
        if half is None or not self.halves:
            return ref
        rows = self.buffer.shape[1] // 2
        return ref.at[pl.ds(half * rows, rows)]

    def copies(self, e):
        out = []
        for i, (axis, step, half, there) in enumerate(SENDS[e]):
            if half == 1 and not self.halves:
                continue
            if axis == "core":
                target, sem = member(self.y, self.z, self.core, 0, 0), self.recv_core.at[e]
                target = target + 1 - 2 * self.core
            else:
                da, db = (step, 0) if axis == "a" else (0, step)
                target = member(self.y, self.z, self.core, da, db)
                sem = self.recv.at[there, half or 0]
            ref = self.block(e, half)
            out.append(
                pltpu.make_async_remote_copy(
                    src_ref=ref,
                    dst_ref=ref,
                    send_sem=self.send.at[FIRST[e] + i],
                    recv_sem=sem,
                    device_id=(self.x, target),
                    device_id_type=MESH,
                )
            )
        return out

    def await_block(self, e):
        if e == 0:
            return
        for half in (0, 1) if split(e) and self.halves else (None,):
            ref = self.block(e, half)
            pltpu.make_async_remote_copy(
                src_ref=ref,
                dst_ref=ref,
                send_sem=self.send.at[0],
                recv_sem=self.recv.at[e, half or 0],
                device_id=(self.x, member(self.y, self.z, self.core, 0, 1)),
                device_id_type=MESH,
            ).wait_recv()

    def await_core(self, e, block):
        ref = self.buffer.at[block]
        pltpu.make_async_remote_copy(
            src_ref=ref,
            dst_ref=ref,
            send_sem=self.send.at[0],
            recv_sem=self.recv_core.at[e],
            device_id=(self.x, member(self.y, self.z, 1 - self.core, 0, 0)),
            device_id_type=MESH,
        ).wait_recv()

    def pass_on(self, e):
        for copy in self.copies(e):
            copy.start()

    def await_sends(self):
        for e in range(CHIPS):
            for copy in self.copies(e):
                copy.wait_send()


def norm_row(meta, block):
    return jnp.concatenate([meta[block, 0:1, 128:256], meta[block, 1:2, 128:256]], axis=1)


def scores_of(vec, rows, norm):
    products = lax.dot_general(
        vec, rows, (((1,), (1,)), ((), ())), preferred_element_type=jnp.float32
    )
    return ((2.0 * products - norm) * FACTOR).astype(jnp.bfloat16)


TILE = 256


def gather_kernel(
    vectors, boundary, centroids, pairs,
    scores, cen, meta, vec_bf, arrived,
    bnd, parts, staged,
    vec_sem,
    bnd_send, bnd_recv, bnd_core,
    meta_send, meta_recv, meta_core,
    cen_send, cen_recv, cen_core,
    x_send, x_recv, own_sem,
):
    where = position()
    x, y, z, core = where
    me = member(y, z, core, 0, 0)
    other = 1 - core

    barrier = pltpu.get_barrier_semaphore()
    greeted = [(x, member(y, z, core, da, db)) for da, db in ((1, 0), (3, 0), (0, 1), (0, 3))]
    greeted += [(x, member(y, z, other, 0, 0))]
    greeted += [((x + dx) % N_GRP, me) for dx in (1, 2, 3)]
    for device in greeted:
        pl.semaphore_signal(barrier, inc=1, device_id=device, device_id_type=MESH)

    fetch = pltpu.make_async_copy(vectors, staged, vec_sem)
    fetch.start()

    bnd[me] = boundary[...].astype(jnp.bfloat16)
    packed = pairs[...]
    owner, slot = packed // CEN, packed % CEN
    device_row = lax.broadcasted_iota(jnp.int32, (DEVICES, 128), 0)
    named = [device_row == owner[k : k + 1, :] for k in range(LIST)]
    marks = sum(jnp.where(n, 1.0, 0.0) for n in named)
    before = lax.broadcasted_iota(jnp.int32, (128, 128), 0)
    column = lax.broadcasted_iota(jnp.int32, (128, 128), 1)
    earlier = jnp.where(before < column % BROWS, 1.0, 0.0).astype(jnp.bfloat16)
    counts = jnp.dot(marks.astype(jnp.bfloat16), earlier, preferred_element_type=jnp.float32)
    places = jnp.concatenate(
        [jnp.sum(jnp.where(n, counts, 0.0), axis=0, keepdims=True) for n in named], axis=0
    )
    code = (owner.astype(jnp.float32) * CAP + places) * FIELD + (slot + 1).astype(jnp.float32)
    lane = lax.broadcasted_iota(jnp.int32, (LIST, 128), 1)
    row = lax.broadcasted_iota(jnp.int32, (LIST, 128), 0)
    meta[me, :, 0:128] = jnp.where(lane // BROWS == core, code, 0.0)

    own = centroids[...]
    cen[me] = own.astype(jnp.bfloat16)
    squares = own * own
    partial = sum(squares[:, i * 128 : (i + 1) * 128] for i in range(D // 128))
    norms = [jnp.sum(partial[i * 128 : (i + 1) * 128].T, axis=0, keepdims=True) for i in range(2)]
    meta[me, :, 128:256] = jnp.where(row == 0, norms[0], jnp.where(row == 1, norms[1], 0.0))

    s_bnd = Stream(bnd, True, bnd_send, bnd_recv, bnd_core, where)
    s_meta = Stream(meta, False, meta_send, meta_recv, meta_core, where)
    s_cen = Stream(cen, True, cen_send, cen_recv, cen_core, where)

    pl.semaphore_wait(barrier, len(greeted))
    s_meta.pass_on(0)
    s_bnd.pass_on(0)
    s_cen.pass_on(0)

    fetch.wait()

    @pl.loop(0, V_DEV // 128)
    def _(t):
        rows = pl.ds(pl.multiple_of(t * 128, 128), 128)
        vec_bf[rows, :] = staged[rows, :].astype(jnp.bfloat16)

    for e in range(1, CHIPS):
        s_meta.await_block(e)
        s_meta.pass_on(e)
        s_bnd.await_block(e)
        s_bnd.pass_on(e)

    @pl.loop(0, CHIPS)
    def _(e):
        da, db = offsets(e)
        block = member(y, z, other, da, db)
        s_meta.await_core(e, block)
        s_bnd.await_core(e, block)

    srow = lax.broadcasted_iota(jnp.int32, (N_GRP * 16, 128), 0)
    scol = lax.broadcasted_iota(jnp.int32, (N_GRP * 16, 128), 1)
    wanted = ((srow // 16) * N_MEM + me) * CAP + srow % CAP
    wanted = jnp.where((srow // CAP) % 2 == scol // BROWS, wanted * FIELD, -(1 << 22))
    wanted = wanted.astype(jnp.float32)
    ones = jnp.ones((128, 128), jnp.bfloat16)

    @pl.loop(0, CHIPS)
    def _(p):
        both = meta[2 * p, :, 0:128] + meta[2 * p + 1, :, 0:128]
        found = jnp.zeros((N_GRP * 16, 128), jnp.float32)
        for k in range(LIST):
            apart = both[k : k + 1, :] - wanted
            found += jnp.where((apart > 0.0) & (apart < FIELD), apart, 0.0)
        pick = jnp.where(found > 0.0, 1.0, 0.0).astype(jnp.bfloat16)
        source = bnd[pl.ds(2 * p, 2)].reshape(128, D)
        rows = jnp.dot(pick, source, preferred_element_type=jnp.float32).astype(jnp.bfloat16)
        slots = jnp.dot(found.astype(jnp.bfloat16), ones, preferred_element_type=jnp.float32)
        slots = slots.astype(jnp.bfloat16)
        for g in range(N_GRP):
            parts[g, p, :, 0:D] = rows[g * 16 : (g + 1) * 16]
            parts[g, p, :, D:WIDE] = slots[g * 16 : (g + 1) * 16]

    def across(dx):
        return pltpu.make_async_remote_copy(
            src_ref=parts.at[(x + dx) % N_GRP],
            dst_ref=arrived.at[x],
            send_sem=x_send.at[dx],
            recv_sem=x_recv.at[dx],
            device_id=((x + dx) % N_GRP, me),
            device_id_type=MESH,
        )

    for dx in (2, 1, 3):
        across(dx).start()
    keep = pltpu.make_async_copy(parts.at[x], arrived.at[x], own_sem)
    keep.start()

    def score(block):
        norm = norm_row(meta, block)

        @pl.loop(0, V_DEV // TILE)
        def _(t):
            rows = pl.ds(pl.multiple_of(t * TILE, TILE), TILE)
            scores[block, rows, :] = scores_of(vec_bf[rows, :], cen[block], norm)

    @pl.loop(0, CHIPS + LAG)
    def _(i):
        for e in range(1, CHIPS):

            @pl.when(i == e)
            def _(e=e):
                s_cen.await_block(e)
                s_cen.pass_on(e)

        @pl.when(i < CHIPS - LATER)
        def _():
            da, db = offsets(i)
            score(member(y, z, core, da, db))

        @pl.when(i >= LAG)
        def _():
            e = i - LAG
            da, db = offsets(e)
            block = member(y, z, other, da, db)
            s_cen.await_core(e, block)

            @pl.when(e < CHIPS - LATER)
            def _():
                score(block)

    for dx in (1, 2, 3):
        pltpu.make_async_remote_copy(
            src_ref=parts.at[x],
            dst_ref=arrived.at[(x - dx + N_GRP) % N_GRP],
            send_sem=x_send.at[dx],
            recv_sem=x_recv.at[dx],
            device_id=((x + dx) % N_GRP, me),
            device_id_type=MESH,
        ).wait_recv()
        across(dx).wait_send()
    keep.wait()
    s_meta.await_sends()
    s_bnd.await_sends()
    s_cen.await_sends()


def finish_kernel(
    scores, cen, meta, vec_bf, arrived, centroids,
    scores_out, residual_out, dist,
    late, residual,
    done_sem, late_sem, residual_sem,
):
    x, y, z, core = position()

    def block_of(e, side):
        da, db = offsets(e)
        return member(y, z, (core + side) % 2, da, db)

    def columns(block):
        return scores_out.at[:, pl.ds(pl.multiple_of(block * CEN, CEN), CEN)]

    def early(i):
        block = block_of(i // 2, i % 2)
        return pltpu.make_async_copy(scores.at[block], columns(block), done_sem.at[i])

    n_early, n_late = 2 * (CHIPS - LATER), 2 * LATER

    @pl.loop(0, n_early)
    def _(i):
        early(i).start()

    def late_copy(i):
        block = block_of(CHIPS - LATER + i // 2, i % 2)
        return pltpu.make_async_copy(late.at[i], columns(block), late_sem.at[i])

    @pl.loop(0, n_late)
    def _(i):
        block = block_of(CHIPS - LATER + i // 2, i % 2)
        norm = norm_row(meta, block)

        @pl.loop(0, V_DEV // TILE)
        def _(t):
            rows = pl.ds(pl.multiple_of(t * TILE, TILE), TILE)
            late[i, rows, :] = scores_of(vec_bf[rows, :], cen[block], norm)

        late_copy(i).start()

    own = centroids[...]
    high = own.astype(jnp.bfloat16)
    rest = own - high.astype(jnp.float32)
    middle = rest.astype(jnp.bfloat16)
    low = (rest - middle.astype(jnp.float32)).astype(jnp.bfloat16)
    lane = lax.broadcasted_iota(jnp.int32, (256, 128), 1).astype(jnp.float32)

    def residual_copy(g):
        rows = pl.ds(g * 256, 256)
        return pltpu.make_async_copy(residual.at[rows], residual_out.at[rows], residual_sem.at[g])

    for g in range(N_GRP):
        got = arrived[g].reshape(256, WIDE)
        slot = got[:, D:WIDE].astype(jnp.float32)
        pick = jnp.concatenate(
            [jnp.where(slot == lane + 1.0, 1.0, 0.0), jnp.where(slot == lane + 129.0, 1.0, 0.0)], axis=1
        ).astype(jnp.bfloat16)
        centre = jnp.dot(pick, high, preferred_element_type=jnp.float32) + (
            jnp.dot(pick, middle, preferred_element_type=jnp.float32)
            + jnp.dot(pick, low, preferred_element_type=jnp.float32)
        )
        value = got[:, 0:D].astype(jnp.float32) - centre
        residual[g * 256 : (g + 1) * 256, :] = value
        residual_copy(g).start()
        squares = value * value
        partial = sum(squares[:, i * 128 : (i + 1) * 128] for i in range(D // 128))
        for i in range(2):
            total = jnp.sum(partial[i * 128 : (i + 1) * 128].T, axis=0, keepdims=True)
            dist[:, (2 * g + i) * 128 : (2 * g + i + 1) * 128] = total / D

    @pl.loop(0, n_early)
    def _(i):
        early(i).wait()

    @pl.loop(0, n_late)
    def _(i):
        late_copy(i).wait()

    for g in range(N_GRP):
        residual_copy(g).wait()


def on_device(vectors, boundary, centroids, list_owner, list_slot):
    packed = (list_owner * CEN + list_slot).T
    pairs = jnp.concatenate([packed, packed], axis=1)
    vmem = pl.BlockSpec(memory_space=pltpu.VMEM)
    hbm = pl.BlockSpec(memory_space=pl.ANY)
    dma = pltpu.SemaphoreType.DMA
    stream = [dma((N_SENDS,)), dma((CHIPS, 2)), dma((CHIPS,))]
    scores, cen, meta, vec_bf, arrived = pl.pallas_call(
        gather_kernel,
        out_shape=(
            pltpu.VMEM((N_MEM, V_DEV, CEN), jnp.bfloat16),
            pltpu.VMEM((N_MEM, CEN, D), jnp.bfloat16),
            pltpu.VMEM((N_MEM, LIST, 256), jnp.float32),
            pltpu.VMEM((V_DEV, D), jnp.bfloat16),
            pltpu.VMEM((N_GRP, CHIPS, 16, WIDE), jnp.bfloat16),
        ),
        in_specs=[hbm, vmem, vmem, vmem],
        out_specs=[vmem] * 5,
        scratch_shapes=[
            pltpu.VMEM((N_MEM, BROWS, D), jnp.bfloat16),
            pltpu.VMEM((N_GRP, CHIPS, 16, WIDE), jnp.bfloat16),
            pltpu.VMEM((V_DEV, D), jnp.float32),
            dma,
            *stream,
            *stream,
            *stream,
            dma((N_GRP,)),
            dma((N_GRP,)),
            dma,
        ],
        compiler_params=pltpu.CompilerParams(
            collective_id=0, has_side_effects=True, vmem_limit_bytes=12 << 20
        ),
        name="gather",
    )(vectors, boundary, centroids, pairs)
    return pl.pallas_call(
        finish_kernel,
        out_shape=(
            jax.ShapeDtypeStruct((V_DEV, N_MEM * CEN), jnp.bfloat16),
            jax.ShapeDtypeStruct((DEVICES * CAP, D), jnp.float32),
            jax.ShapeDtypeStruct((1, DEVICES * CAP), jnp.float32),
        ),
        in_specs=[vmem] * 6,
        out_specs=[hbm, hbm, vmem],
        scratch_shapes=[
            pltpu.VMEM((2 * LATER, V_DEV, CEN), jnp.bfloat16),
            pltpu.VMEM((DEVICES * CAP, D), jnp.float32),
            dma((2 * (CHIPS - LATER),)),
            dma((2 * LATER,)),
            dma((N_GRP,)),
        ],
        compiler_params=pltpu.CompilerParams(vmem_limit_bytes=12 << 20),
        name="finish",
    )(scores, cen, meta, vec_bf, arrived, centroids)


def solution(mesh):
    spec = P(("grp", "mem"), None)
    return jax.shard_map(
        on_device,
        mesh=mesh,
        in_specs=(spec,) * 5,
        out_specs=(spec,) * 3,
        check_vma=False,
    )
```

time: 123 us -> 95 us (0.77)
  Pallas kernels: 0 us -> 89.4 us
  blocking collectives: 41.2 us -> 0 us
  matrix products: 19.7 us -> 0 us
  starting transfers between devices: 19.5 us -> 0 us
  between operations: 14.2 us -> 0.64 us
  local copies, waits for them, and re-layouts: 15.1 us -> 3.95 us
  other arithmetic: 11.1 us -> 0.78 us
  waiting for transfers between devices: 1.94 us -> 0 us
    pallas_call x0 -> x2, Pallas kernels: none -> 89.4 us  [the longest x1 74.2 us: on_device(): pl.pallas_call(gather_kernel, out_shape=(pltpu.VMEM((N_MEM, V_DEV, CEN),...]
    all_gather x1 -> x0, blocking collectives: 41.2 us -> none  [on_device(): panel_norms = lax.all_gather(cen_norm, 'mem', axis=0, tiled=True)]
    dot_general x1 -> x0, matrix products: 19.7 us -> none  [on_device(): lax.dot_general(vec_bf, panel_rows, contract, preferred_element_type=jnp....]
    all_to_all x2 -> x0, starting transfers between devices: 19.4 us -> none  [the longest x1 11.5 us: on_device(): lax.all_to_all(slot_buffer.reshape(devices, capacity).astype(jnp.bfloat16...]
    reduce_sum x3 -> x0, other arithmetic: 6.85 us -> none  [the longest x1 4.26 us: on_device(): residual, distance = (residual, jnp.sum(residual * residual, axis=-1) / D)]
    scatter x2 -> x0, local copies, waits for them, and re-layouts: 6.61 us -> none  [the longest x1 4.17 us: on_device(): jnp.zeros((devices * capacity, D), jnp.float32).at[target].set(sent_rows)]
    gather x1 -> x0, local copies, waits for them, and re-layouts: 5.23 us -> none  [on_device(): centre = centroids[jnp.maximum(slot_index, 0)]]
    convert_element_type x3 -> x0, other arithmetic: 3.27 us -> none  [the longest x1 3.26 us: on_device(): vec_buffer.reshape(devices, capacity, D).astype(jnp.bfloat16)]
  transfers between devices with their start and end apart: 3 -> 0, of which waited for: 1 -> 0; matrix products, arithmetic and copies ran while one was open for 19% -> 0% of each run, Pallas kernels for 0% -> 0%
where the time goes in v1:
time: 95 us; the launch traced here: 94.8 us
  Pallas kernels  89.4 us (94%)
  local copies, waits for them, and re-layouts  3.95 us (4%)
    pallas_call x1, Pallas kernels, on_device(): pl.pallas_call(gather_kernel, out_shape=(pltpu.VMEM((N_MEM, V_DEV, CEN),...  74.2 us
    pallas_call x1, Pallas kernels, on_device(): pl.pallas_call(finish_kernel, out_shape=(jax.ShapeDtypeStruct((V_DEV, N_M...  15.2 us
    unnamed x6, local copies, waits for them, and re-layouts  3.95 us

profile of v1, /device:TPU:1, one launch (start us, length us, event | category | flops | bytes accessed | tf_op | source)
XLA Modules:
  0.0 94.8 jit_solution(6838533478334977918)
XLA Ops:
  0.6 0.7 add_bitcast_fusion
  1.3 0.1 pad_add_fusion.pairs
  1.4 0.0 copy-start
  1.4 1.9 %copy-done = f32[1024,768]{1,0:T(8,128)S(1)} copy-done((f32[1024,768]{1,0:T(8,128)S(1)}, f32[1024,768]{1,0:T(8,128)}, u32[]{:S(2)}) %copy-start) | copy-done | bytes 3145752
  3.3 0.0 copy-start.1
  3.3 1.1 %copy-done.1 = f32[256,768]{1,0:T(8,128)S(1)} copy-done((f32[256,768]{1,0:T(8,128)S(1)}, f32[256,768]{1,0:T(8,128)}, u32[]{:S(2)}) %copy-start.1) | copy-done | bytes 786456
  4.4 0.0 copy-start.2
  4.4 0.9 copy-done.2
  5.4 74.2 %gather.1 = (bf16[32,1024,256]{2,1,0:T(8,128)(2,1)S(1)}, bf16[32,256,768]{2,1,0:T(8,128)(2,1)S(1)}, f32[32,8,256]{2,1,0:T(8,128)S(1)}, bf16[1024,768]{1,0:T(8,128)(2,1)S(1)}, bf16[4,16,16,896]{3,2,1,0:T(8,128)(2,1)S(1)}) custom-call(f32[1024,768]{1,0:T(8,128)S(1)} %copy-done, f32[64,768]{1,0:T(8,128)S(1)} %copy-done.2, f32[256,768]{1,0:T(8,128)S(1)} %copy-done.1, ...), custom_call_target="tpu_custom_call" | custom-call | tf_op jit(solution)/shard_map/gather/pallas_call | solution.py:425
  79.6 15.2 %finish.1 = (bf16[1024,8192]{1,0:T(8,128)(2,1)}, f32[1024,768]{1,0:T(8,128)}, f32[1,1024]{1,0:T(1,128)}) custom-call(bf16[32,1024,256]{2,1,0:T(8,128)(2,1)S(1)} %get-tuple-element.8.scores, bf16[32,256,768]{2,1,0:T(8,128)(2,1)S(1)} %get-tuple-element.9.cen, f32[32,8,256]{2,1,0:T(8,128)S(1)} %get-tuple-element.10.meta, ...), custom_call_target="tpu_custom_call" | custom-call | tf_op jit(solution)/shard_map/finish/pallas_call | solution.py:453
Async XLA Ops:
  1.4 1.9 %copy-start = (f32[1024,768]{1,0:T(8,128)S(1)}, f32[1024,768]{1,0:T(8,128)}, u32[]{:S(2)}) copy-start(f32[1024,768]{1,0:T(8,128)} %vectors.1) | copy-start | bytes 9437188
  3.3 1.1 %copy-start.1 = (f32[256,768]{1,0:T(8,128)S(1)}, f32[256,768]{1,0:T(8,128)}, u32[]{:S(2)}) copy-start(f32[256,768]{1,0:T(8,128)} %centroids.3) | copy-start | bytes 2359300
  4.4 0.9 copy-start.2

commit v2 on v1

v2 whole, which is shorter than its diff:
```python
import functools
import math

import jax
import jax.numpy as jnp
from jax import lax
from jax.experimental import pallas as pl
from jax.experimental.pallas import tpu as pltpu
from jax.sharding import PartitionSpec as P

D = 768
LIST = 8
CAP = 8
BROWS = 64
WIDE = D + 128
CEN = 256
V_DEV = 1024
N_GRP = 4
N_MEM = 32
RING = 4
CHIPS = 16
DEVICES = 128
FIELD = 512
MESH = pl.DeviceIdType.MESH
FACTOR = 1.0 / math.sqrt(D)
FIRST_AT, SECOND_AT = 8, 14
ROWS_LAG = 2
LATER = 2
LAG = 2
RESIDUALS_AT = 13

ORDER = (
    (0, 0), (3, 0), (1, 0), (0, 3), (0, 1), (2, 0), (3, 3), (3, 1),
    (1, 3), (1, 1), (0, 2), (2, 3), (2, 1), (3, 2), (1, 2), (2, 2),
)
PLACE = {offset: e for e, offset in enumerate(ORDER)}


def known(e):
    da, db = ORDER[e]
    return max(e, PLACE[db, da])


def sends_of(e):
    da, db = ORDER[e]
    out = []
    if db == 0:
        if da == 0:
            out += [("a", 1, None, PLACE[3, 0]), ("a", 3, None, PLACE[1, 0])]
        elif da == 3:
            out += [("a", 1, 0, PLACE[2, 0])]
        elif da == 1:
            out += [("a", 3, 1, PLACE[2, 0])]
        out += [("b", 1, None, PLACE[da, 3]), ("b", 3, None, PLACE[da, 1])]
    elif db == 3:
        out += [("b", 1, 0, PLACE[da, 2])]
    elif db == 1:
        out += [("b", 3, 1, PLACE[da, 2])]
    return out + [("core", 0, None, e)]


SENDS = [sends_of(e) for e in range(CHIPS)]
FIRST = [sum(len(s) for s in SENDS[:e]) for e in range(CHIPS)]
N_SENDS = sum(len(s) for s in SENDS)


def split(order):
    da, db = ORDER[order]
    return db == 2 or (db == 0 and da == 2)


def position():
    m = lax.axis_index("mem")
    return lax.axis_index("grp"), m // 8, (m // 2) % RING, m % 2


def member(y, z, core, da, db):
    dy = (1 - core) * da + core * db
    dz = (1 - core) * db + core * da
    return (((y + dy) % RING) * RING + (z + dz) % RING) * 2 + core


def offsets(e):
    da = sum(jnp.where(e == k, o[0], 0) for k, o in enumerate(ORDER))
    db = sum(jnp.where(e == k, o[1], 0) for k, o in enumerate(ORDER))
    return da, db


class Stream:
    def __init__(self, buffer, send, recv, recv_core, where):
        self.buffer = buffer
        self.send, self.recv, self.recv_core = send, recv, recv_core
        self.x, self.y, self.z, self.core = where

    def block(self, e, half):
        da, db = ORDER[e]
        ref = self.buffer.at[member(self.y, self.z, self.core, da, db)]
        if half is None:
            return ref
        rows = self.buffer.shape[1] // 2
        return ref.at[pl.ds(half * rows, rows)]

    def copies(self, e, axes=("a", "b", "core")):
        out = []
        for i, (axis, step, half, there) in enumerate(SENDS[e]):
            if axis not in axes:
                continue
            if axis == "core":
                target, sem = member(self.y, self.z, self.core, 0, 0), self.recv_core.at[e]
                target = target + 1 - 2 * self.core
            else:
                da, db = (step, 0) if axis == "a" else (0, step)
                target = member(self.y, self.z, self.core, da, db)
                sem = self.recv.at[there, half or 0]
            ref = self.block(e, half)
            copy = pltpu.make_async_remote_copy(
                src_ref=ref,
                dst_ref=ref,
                send_sem=self.send.at[FIRST[e] + i],
                recv_sem=sem,
                device_id=(self.x, target),
                device_id_type=MESH,
            )
            out.append(copy)
        return out

    def await_block(self, e):
        if e == 0:
            return
        for half in (0, 1) if split(e) else (None,):
            ref = self.block(e, half)
            pltpu.make_async_remote_copy(
                src_ref=ref,
                dst_ref=ref,
                send_sem=self.send.at[0],
                recv_sem=self.recv.at[e, half or 0],
                device_id=(self.x, member(self.y, self.z, self.core, 0, 1)),
                device_id_type=MESH,
            ).wait_recv()

    def await_core(self, e, block):
        ref = self.buffer.at[block]
        pltpu.make_async_remote_copy(
            src_ref=ref,
            dst_ref=ref,
            send_sem=self.send.at[0],
            recv_sem=self.recv_core.at[e],
            device_id=(self.x, member(self.y, self.z, 1 - self.core, 0, 0)),
            device_id_type=MESH,
        ).wait_recv()

    def pass_on(self, e, axes=("a", "b", "core")):
        for copy in self.copies(e, axes):
            copy.start()

    def await_sends(self):
        for e in range(CHIPS):
            for copy in self.copies(e):
                copy.wait_send()


def norm_row(bnd, block):
    part = bnd[block, 16:32, D:WIDE].astype(jnp.float32)
    both = part[8:10] + (part[10:12] + part[12:14])
    return jnp.concatenate([both[0:1], both[1:2]], axis=1)


def scores_of(vec, rows, norm):
    products = lax.dot_general(
        vec, rows, (((1,), (1,)), ((), ())), preferred_element_type=jnp.float32
    )
    return (products * (2.0 * FACTOR) - norm).astype(jnp.bfloat16)


TILE = 1024


def gather_kernel(
    vectors, boundary, centroids, owners, slots,
    scores, cen, bnd, vec_bf, residual, dist,
    parts, arrived, kept, part_slots, arrived_slots, rows_in, centre_in, owners_in, slots_in,
    in_sem,
    bnd_send, bnd_recv, bnd_core,
    cen_send, cen_recv, cen_core,
    x_send, x_recv, own_sem,
):
    where = position()
    x, y, z, core = where
    me = member(y, z, core, 0, 0)
    other = 1 - core

    barrier = pltpu.get_barrier_semaphore()
    greeted = [(x, member(y, z, core, da, db)) for da, db in ((1, 0), (3, 0), (0, 1), (0, 3))]
    greeted += [(x, member(y, z, other, 0, 0))]
    greeted += [((x + dx) % N_GRP, me) for dx in (1, 2, 3)]
    for device in greeted:
        pl.semaphore_signal(barrier, inc=1, device_id=device, device_id_type=MESH)

    fetches = [
        pltpu.make_async_copy(source, target, in_sem.at[i])
        for i, (source, target) in enumerate(
            ((centroids, centre_in), (owners, owners_in), (slots, slots_in), (boundary, rows_in), (vectors, residual))
        )
    ]
    for fetch in fetches:
        fetch.start()

    s_bnd = Stream(bnd, bnd_send, bnd_recv, bnd_core, where)
    s_cen = Stream(cen, cen_send, cen_recv, cen_core, where)

    fetches[0].wait()
    own = centre_in[...]
    cen[me] = own.astype(jnp.bfloat16)
    pl.semaphore_wait(barrier, len(greeted))

    fetches[1].wait()
    fetches[2].wait()
    owner = jnp.concatenate([owners_in[...]] * 2, axis=1)
    slot = jnp.concatenate([slots_in[...]] * 2, axis=1)
    device_row = lax.broadcasted_iota(jnp.int32, (DEVICES, 128), 0)
    named = [device_row == owner[k : k + 1, :] for k in range(LIST)]
    marks = sum(jnp.where(n, 1.0, 0.0) for n in named)
    before = lax.broadcasted_iota(jnp.int32, (128, 128), 0)
    column = lax.broadcasted_iota(jnp.int32, (128, 128), 1)
    earlier = jnp.where(before < column % BROWS, 1.0, 0.0).astype(jnp.bfloat16)
    counts = jnp.dot(marks.astype(jnp.bfloat16), earlier, preferred_element_type=jnp.float32)
    places = jnp.concatenate(
        [jnp.sum(jnp.where(n, counts, 0.0), axis=0, keepdims=True) for n in named], axis=0
    )
    lane = lax.broadcasted_iota(jnp.int32, (LIST, 128), 1)
    lists = [
        jnp.where(lane // BROWS == core, a, 0.0)
        for a in (owner.astype(jnp.float32), places, (slot + 1).astype(jnp.float32))
    ]
    squares = own * own
    partial = sum(squares[:, i * 128 : (i + 1) * 128] for i in range(D // 128))
    norms = [jnp.sum(partial[i * 128 : (i + 1) * 128].T, axis=0, keepdims=True) for i in range(2)]
    norm = jnp.concatenate(norms, axis=0) * FACTOR
    high = norm.astype(jnp.bfloat16).astype(jnp.float32)
    middle = (norm - high).astype(jnp.bfloat16).astype(jnp.float32)
    low = norm - high - middle
    info = [*lists, high, middle, low, jnp.zeros((BROWS - 3 * LIST - 6, 128), jnp.float32)]
    bnd[me, :, D:WIDE] = jnp.concatenate(info, axis=0).astype(jnp.bfloat16)
    fetches[3].wait()
    bnd[me, :, 0:D] = rows_in[...].astype(jnp.bfloat16)

    s_bnd.pass_on(0)

    fetches[4].wait()

    @pl.loop(0, V_DEV // 128)
    def _(t):
        rows = pl.ds(pl.multiple_of(t * 128, 128), 128)
        vec_bf[rows, :] = residual[rows, :].astype(jnp.bfloat16)

    srow = lax.broadcasted_iota(jnp.int32, (N_GRP * 16, 128), 0)
    scol = lax.broadcasted_iota(jnp.int32, (N_GRP * 16, 128), 1)
    wanted = ((srow // 16) * N_MEM + me) * CAP + srow % CAP
    wanted = jnp.where((srow // CAP) % 2 == scol // BROWS, wanted * FIELD, -(1 << 22))
    wanted = wanted.astype(jnp.float32)
    ones = jnp.ones((128, 128), jnp.bfloat16)

    place = lax.broadcasted_iota(jnp.int32, (N_GRP * 16, 128), 1)

    def select(e):
        da, db = ORDER[e]
        p = member(y, z, core, da, db) // 2
        s_bnd.await_core(PLACE[db, da], 2 * p + other)
        info = bnd[2 * p, 0:32, D:WIDE].astype(jnp.float32) + bnd[2 * p + 1, 0:32, D:WIDE].astype(jnp.float32)
        both = (info[0:8] * CAP + info[8:16]) * FIELD + info[16:24]
        found = jnp.zeros((N_GRP * 16, 128), jnp.float32)
        for k in range(LIST):
            apart = both[k : k + 1, :] - wanted
            found += jnp.where((apart > 0.0) & (apart < FIELD), apart, 0.0)
        pick = jnp.where(found > 0.0, 1.0, 0.0).astype(jnp.bfloat16)
        source = bnd[pl.ds(2 * p, 2), :, 0:D].reshape(128, D)
        rows = jnp.dot(pick, source, preferred_element_type=jnp.float32).astype(jnp.bfloat16)
        for g in range(N_GRP):
            parts[g, p] = rows[g * 16 : (g + 1) * 16]
        for dx in (2, 1, 3):
            pltpu.make_async_remote_copy(
                src_ref=parts.at[(x + dx) % N_GRP, p],
                dst_ref=arrived.at[x, p],
                send_sem=x_send.at[dx, 0],
                recv_sem=x_recv.at[dx, 0],
                device_id=((x + dx) % N_GRP, me),
                device_id_type=MESH,
            ).start()
        number = jnp.dot(found.astype(jnp.bfloat16), ones, preferred_element_type=jnp.float32)
        kept[...] += jnp.where(place == p, number, 0.0)

    kept[...] = jnp.zeros_like(kept)
    for step in range(CHIPS + ROWS_LAG):
        if 0 < step < CHIPS:
            s_bnd.await_block(step)
            s_bnd.pass_on(step)
        if step == FIRST_AT:
            s_cen.pass_on(0, ("a", "core"))
        if step == SECOND_AT:
            s_cen.pass_on(0, ("b",))
        for e in range(CHIPS):
            if known(e) == step - ROWS_LAG:
                select(e)
    for g in range(N_GRP):
        part_slots[g] = kept[g * 16 : (g + 1) * 16].astype(jnp.bfloat16)

    def across(dx, i, arriving):
        to = (x + dx) % N_GRP
        origin = (x - dx + N_GRP) % N_GRP if arriving else x
        a, b = ((parts, arrived), (part_slots, arrived_slots))[i]
        return pltpu.make_async_remote_copy(
            src_ref=a.at[to],
            dst_ref=b.at[origin],
            send_sem=x_send.at[dx, i],
            recv_sem=x_recv.at[dx, i],
            device_id=(to, me),
            device_id_type=MESH,
        )

    for dx in (2, 1, 3):
        across(dx, 1, False).start()
    keeps = [
        pltpu.make_async_copy(a.at[x], b.at[x], own_sem.at[i])
        for i, (a, b) in enumerate(((parts, arrived), (part_slots, arrived_slots)))
    ]
    for keep in keeps:
        keep.start()

    def residuals():
        for dx in (1, 2, 3):
            for i in (0, 1):
                across(dx, i, True).wait_recv()
        for keep in keeps:
            keep.wait()
        own = centre_in[...]
        high = own.astype(jnp.bfloat16)
        rest = own - high.astype(jnp.float32)
        middle = rest.astype(jnp.bfloat16)
        low = (rest - middle.astype(jnp.float32)).astype(jnp.bfloat16)
        lane = lax.broadcasted_iota(jnp.int32, (256, 128), 1)
        pair = lax.broadcasted_iota(jnp.int32, (256, 128), 0) // 16
        at = lane.astype(jnp.float32)
        for g in range(N_GRP):
            numbers = jnp.concatenate([arrived_slots[g].astype(jnp.float32)] * CHIPS, axis=0)
            numbers = jnp.where(lane == pair, numbers, 0.0).astype(jnp.bfloat16)
            number = jnp.dot(numbers, ones, preferred_element_type=jnp.float32)
            pick = jnp.concatenate(
                [jnp.where(number == at + 1.0, 1.0, 0.0), jnp.where(number == at + 129.0, 1.0, 0.0)], axis=1
            ).astype(jnp.bfloat16)
            centre = jnp.dot(pick, high, preferred_element_type=jnp.float32) + (
                jnp.dot(pick, middle, preferred_element_type=jnp.float32)
                + jnp.dot(pick, low, preferred_element_type=jnp.float32)
            )
            value = arrived[g].reshape(256, D).astype(jnp.float32) - centre
            residual[g * 256 : (g + 1) * 256, :] = value
            squares = value * value
            partial = sum(squares[:, i * 128 : (i + 1) * 128] for i in range(D // 128))
            for i in range(2):
                total = jnp.sum(partial[i * 128 : (i + 1) * 128].T, axis=0, keepdims=True)
                dist[:, (2 * g + i) * 128 : (2 * g + i + 1) * 128] = total / D

    def score(block):
        norm = norm_row(bnd, block)

        @pl.loop(0, V_DEV // TILE)
        def _(t):
            rows = pl.ds(pl.multiple_of(t * TILE, TILE), TILE)
            scores[block, rows, :] = scores_of(vec_bf[rows, :], cen[block], norm)

    @pl.loop(0, CHIPS + LAG)
    def _(i):
        for e in range(1, CHIPS):

            @pl.when(i == e)
            def _(e=e):
                s_cen.await_block(e)
                s_cen.pass_on(e)

        @pl.when(i == RESIDUALS_AT)
        def _():
            residuals()

        @pl.when(i < CHIPS - LATER)
        def _():
            da, db = offsets(i)
            score(member(y, z, core, da, db))

        @pl.when(i >= LAG)
        def _():
            e = i - LAG
            da, db = offsets(e)
            block = member(y, z, other, da, db)
            s_cen.await_core(e, block)

            @pl.when(e < CHIPS - LATER)
            def _():
                score(block)

    for dx in (1, 2, 3):
        for i in (0, 1):
            across(dx, i, False).wait_send()
    s_bnd.await_sends()
    s_cen.await_sends()


def finish_kernel(
    scores, cen, bnd, vec_bf, residual, dist,
    scores_out, residual_out, dist_out,
    late,
    done_sem, late_sem, residual_sem,
):
    x, y, z, core = position()

    def block_of(e, side):
        da, db = offsets(e)
        return member(y, z, (core + side) % 2, da, db)

    def columns(block):
        return scores_out.at[:, pl.ds(pl.multiple_of(block * CEN, CEN), CEN)]

    def early(i):
        block = block_of(i // 2, i % 2)
        return pltpu.make_async_copy(scores.at[block], columns(block), done_sem.at[i])

    n_early, n_late = 2 * (CHIPS - LATER), 2 * LATER

    @pl.loop(0, n_early)
    def _(i):
        early(i).start()

    rows_copies = [
        pltpu.make_async_copy(residual, residual_out, residual_sem.at[0]),
        pltpu.make_async_copy(dist, dist_out, residual_sem.at[1]),
    ]
    for copy in rows_copies:
        copy.start()

    def late_copy(i):
        block = block_of(CHIPS - LATER + i // 2, i % 2)
        return pltpu.make_async_copy(late.at[i], columns(block), late_sem.at[i])

    @pl.loop(0, n_late)
    def _(i):
        block = block_of(CHIPS - LATER + i // 2, i % 2)
        norm = norm_row(bnd, block)

        @pl.loop(0, V_DEV // TILE)
        def _(t):
            rows = pl.ds(pl.multiple_of(t * TILE, TILE), TILE)
            late[i, rows, :] = scores_of(vec_bf[rows, :], cen[block], norm)

        late_copy(i).start()

    @pl.loop(0, n_early)
    def _(i):
        early(i).wait()

    @pl.loop(0, n_late)
    def _(i):
        late_copy(i).wait()

    for copy in rows_copies:
        copy.wait()


def on_device(vectors, boundary, centroids, list_owner, list_slot):
    vmem = pl.BlockSpec(memory_space=pltpu.VMEM)
    hbm = pl.BlockSpec(memory_space=pltpu.HBM)
    dma = pltpu.SemaphoreType.DMA
    stream = [dma((N_SENDS,)), dma((CHIPS, 2)), dma((CHIPS,))]
    arrays = (vectors, boundary, centroids, list_owner.T, list_slot.T)
    scores, cen, bnd, vec_bf, residual, dist = pl.pallas_call(
        gather_kernel,
        out_shape=(
            pltpu.VMEM((N_MEM, V_DEV, CEN), jnp.bfloat16),
            pltpu.VMEM((N_MEM, CEN, D), jnp.bfloat16),
            pltpu.VMEM((N_MEM, BROWS, WIDE), jnp.bfloat16),
            pltpu.VMEM((V_DEV, D), jnp.bfloat16),
            pltpu.VMEM((V_DEV, D), jnp.float32),
            pltpu.VMEM((1, DEVICES * CAP), jnp.float32),
        ),
        in_specs=[hbm] * 5,
        out_specs=[vmem] * 6,
        scratch_shapes=[
            pltpu.VMEM((N_GRP, CHIPS, 16, D), jnp.bfloat16),
            pltpu.VMEM((N_GRP, CHIPS, 16, D), jnp.bfloat16),
            pltpu.VMEM((N_GRP * 16, 128), jnp.float32),
            pltpu.VMEM((N_GRP, 16, 128), jnp.bfloat16),
            pltpu.VMEM((N_GRP, 16, 128), jnp.bfloat16),
            pltpu.VMEM((BROWS, D), jnp.float32),
            pltpu.VMEM((CEN, D), jnp.float32),
            pltpu.VMEM((LIST, BROWS), jnp.int32),
            pltpu.VMEM((LIST, BROWS), jnp.int32),
            dma((5,)),
            *stream,
            *stream,
            dma((N_GRP, 2)),
            dma((N_GRP, 2)),
            dma((2,)),
        ],
        compiler_params=pltpu.CompilerParams(
            collective_id=0, has_side_effects=True, vmem_limit_bytes=10 << 20
        ),
        name="gather",
    )(*[pltpu.with_memory_space_constraint(a, pltpu.HBM) for a in arrays])
    return pl.pallas_call(
        finish_kernel,
        out_shape=(
            jax.ShapeDtypeStruct((V_DEV, N_MEM * CEN), jnp.bfloat16),
            jax.ShapeDtypeStruct((DEVICES * CAP, D), jnp.float32),
            jax.ShapeDtypeStruct((1, DEVICES * CAP), jnp.float32),
        ),
        in_specs=[vmem] * 6,
        out_specs=[hbm] * 3,
        scratch_shapes=[
            pltpu.VMEM((2 * LATER, V_DEV, CEN), jnp.bfloat16),
            dma((2 * (CHIPS - LATER),)),
            dma((2 * LATER,)),
            dma((2,)),
        ],
        compiler_params=pltpu.CompilerParams(vmem_limit_bytes=10 << 20),
        name="finish",
    )(scores, cen, bnd, vec_bf, residual, dist)


def solution(mesh):
    spec = P(("grp", "mem"), None)
    return jax.shard_map(
        on_device,
        mesh=mesh,
        in_specs=(spec,) * 5,
        out_specs=(spec,) * 3,
        check_vma=False,
    )
```

time: 95 us -> 66.9 us (0.70)
  Pallas kernels: 89.4 us -> 66.1 us
  local copies, waits for them, and re-layouts: 3.95 us -> 0 us
    pallas_call x1, Pallas kernels: 74.2 us -> 59 us  [on_device(): pl.pallas_call(gather_kernel, out_shape=(pltpu.VMEM((N_MEM, V_DEV, CEN),...]
    pallas_call x1, Pallas kernels: 15.2 us -> 7.11 us  [on_device(): pl.pallas_call(finish_kernel, out_shape=(jax.ShapeDtypeStruct((V_DEV, N_M...]
    unnamed x6 -> x0, local copies, waits for them, and re-layouts: 3.95 us -> none
where the time goes in v2:
time: 66.9 us; the launch traced here: 66.8 us
  Pallas kernels  66.1 us (99%)
    pallas_call x1, Pallas kernels, on_device(): pl.pallas_call(gather_kernel, out_shape=(pltpu.VMEM((N_MEM, V_DEV, CEN),...  59 us
    pallas_call x1, Pallas kernels, on_device(): pl.pallas_call(finish_kernel, out_shape=(jax.ShapeDtypeStruct((V_DEV, N_M...  7.11 us

profile of v2, /device:TPU:1, one launch (start us, length us, event | category | flops | bytes accessed | tf_op | source)
XLA Modules:
  0.0 66.8 jit_solution(13816684922822967487)
XLA Ops:
  0.6 59.0 %gather.1 = (bf16[32,1024,256]{2,1,0:T(8,128)(2,1)S(1)}, bf16[32,256,768]{2,1,0:T(8,128)(2,1)S(1)}, bf16[32,64,896]{2,1,0:T(8,128)(2,1)S(1)}, bf16[1024,768]{1,0...) custom-call(f32[1024,768]{1,0:T(8,128)} %vectors.1, f32[64,768]{1,0:T(8,128)} %boundary.1, ...), custom_call_target="tpu_custom_call" | custom-call | tf_op jit(solution)/shard_map/gather/pallas_call | solution.py:472
  59.6 7.1 %finish.1 = (bf16[1024,8192]{1,0:T(8,128)(2,1)}, f32[1024,768]{1,0:T(8,128)}, f32[1,1024]{1,0:T(1,128)}) custom-call(bf16[32,1024,256]{2,1,0:T(8,128)(2,1)S(1)} %get-tuple-element.9.scores, bf16[32,256,768]{2,1,0:T(8,128)(2,1)S(1)} %get-tuple-element.10.cen, bf16[32,64,896]{2,1,0:T(8,128)(2,1)S(1)} %get-tuple-element.11.bnd, ...), custom_call_target="tpu_custom_call" | custom-call | tf_op jit(solution)/shard_map/finish/pallas_call | solution.py:506

commit v3 on v2

--- a/solution.py
+++ b/solution.py
@@ -23,9 +23,9 @@
 FIELD = 512
 MESH = pl.DeviceIdType.MESH
 FACTOR = 1.0 / math.sqrt(D)
-FIRST_AT, SECOND_AT = 8, 14
+OWN_AT = (("a", 0, 4), ("a", 1, 7), ("b", 0, 10), ("b", 1, 13), ("core", None, 13))
 ROWS_LAG = 2
-LATER = 2
+LATER = 4
 LAG = 2
 RESIDUALS_AT = 13
 
@@ -46,12 +46,13 @@
     out = []
     if db == 0:
         if da == 0:
-            out += [("a", 1, None, PLACE[3, 0]), ("a", 3, None, PLACE[1, 0])]
+            out += [("a", 1, h, PLACE[3, 0]) for h in (0, 1)] + [("a", 3, h, PLACE[1, 0]) for h in (0, 1)]
         elif da == 3:
             out += [("a", 1, 0, PLACE[2, 0])]
         elif da == 1:
             out += [("a", 3, 1, PLACE[2, 0])]
-        out += [("b", 1, None, PLACE[da, 3]), ("b", 3, None, PLACE[da, 1])]
+        for half in (0, 1) if da == 0 else (None,):
+            out += [("b", 1, half, PLACE[da, 3]), ("b", 3, half, PLACE[da, 1])]
     elif db == 3:
         out += [("b", 1, 0, PLACE[da, 2])]
     elif db == 1:
@@ -66,18 +67,18 @@
 
 def split(order):
     da, db = ORDER[order]
-    return db == 2 or (db == 0 and da == 2)
+    return db == 2 or (db == 0 and da == 2) or 0 in (da, db) and 2 not in (da, db)
 
 
 def position():
     m = lax.axis_index("mem")
-    return lax.axis_index("grp"), m // 8, (m // 2) % RING, m % 2
+    return lax.axis_index("grp"), lax.div(m, 8), lax.rem(lax.div(m, 2), RING), lax.rem(m, 2)
 
 
 def member(y, z, core, da, db):
     dy = (1 - core) * da + core * db
     dz = (1 - core) * db + core * da
-    return (((y + dy) % RING) * RING + (z + dz) % RING) * 2 + core
+    return (lax.rem(y + dy, RING) * RING + lax.rem(z + dz, RING)) * 2 + core
 
 
 def offsets(e):
@@ -87,30 +88,28 @@
 
 
 class Stream:
-    def __init__(self, buffer, send, recv, recv_core, where):
+    def __init__(self, buffer, send, recv, recv_core, where, ids):
         self.buffer = buffer
         self.send, self.recv, self.recv_core = send, recv, recv_core
         self.x, self.y, self.z, self.core = where
+        self.ids = ids
 
     def block(self, e, half):
-        da, db = ORDER[e]
-        ref = self.buffer.at[member(self.y, self.z, self.core, da, db)]
+        ref = self.buffer.at[self.ids[ORDER[e]]]
         if half is None:
             return ref
         rows = self.buffer.shape[1] // 2
         return ref.at[pl.ds(half * rows, rows)]
 
-    def copies(self, e, axes=("a", "b", "core")):
+    def copies(self, e, axes=("a", "b", "core"), halves=(None, 0, 1)):
         out = []
         for i, (axis, step, half, there) in enumerate(SENDS[e]):
-            if axis not in axes:
+            if axis not in axes or half not in halves:
                 continue
             if axis == "core":
-                target, sem = member(self.y, self.z, self.core, 0, 0), self.recv_core.at[e]
-                target = target + 1 - 2 * self.core
+                target, sem = self.ids[0, 0] + 1 - 2 * self.core, self.recv_core.at[e]
             else:
-                da, db = (step, 0) if axis == "a" else (0, step)
-                target = member(self.y, self.z, self.core, da, db)
+                target = self.ids[(step, 0) if axis == "a" else (0, step)]
                 sem = self.recv.at[there, half or 0]
             ref = self.block(e, half)
             copy = pltpu.make_async_remote_copy(
@@ -134,7 +133,7 @@
                 dst_ref=ref,
                 send_sem=self.send.at[0],
                 recv_sem=self.recv.at[e, half or 0],
-                device_id=(self.x, member(self.y, self.z, self.core, 0, 1)),
+                device_id=(self.x, self.ids[0, 1]),
                 device_id_type=MESH,
             ).wait_recv()
 
@@ -145,12 +144,12 @@
             dst_ref=ref,
             send_sem=self.send.at[0],
             recv_sem=self.recv_core.at[e],
-            device_id=(self.x, member(self.y, self.z, 1 - self.core, 0, 0)),
+            device_id=(self.x, self.ids[0, 0] + 1 - 2 * self.core),
             device_id_type=MESH,
         ).wait_recv()
 
-    def pass_on(self, e, axes=("a", "b", "core")):
-        for copy in self.copies(e, axes):
+    def pass_on(self, e, axes=("a", "b", "core"), halves=(None, 0, 1)):
+        for copy in self.copies(e, axes, halves):
             copy.start()
 
     def await_sends(self):
@@ -186,13 +185,14 @@
 ):
     where = position()
     x, y, z, core = where
-    me = member(y, z, core, 0, 0)
+    ids = {offset: member(y, z, core, *offset) for offset in ORDER}
+    me = ids[0, 0]
     other = 1 - core
 
     barrier = pltpu.get_barrier_semaphore()
     greeted = [(x, member(y, z, core, da, db)) for da, db in ((1, 0), (3, 0), (0, 1), (0, 3))]
     greeted += [(x, member(y, z, other, 0, 0))]
-    greeted += [((x + dx) % N_GRP, me) for dx in (1, 2, 3)]
+    greeted += [(lax.rem(x + dx, N_GRP), me) for dx in (1, 2, 3)]
     for device in greeted:
         pl.semaphore_signal(barrier, inc=1, device_id=device, device_id_type=MESH)
 
@@ -205,8 +205,8 @@
     for fetch in fetches:
         fetch.start()
 
-    s_bnd = Stream(bnd, bnd_send, bnd_recv, bnd_core, where)
-    s_cen = Stream(cen, cen_send, cen_recv, cen_core, where)
+    s_bnd = Stream(bnd, bnd_send, bnd_recv, bnd_core, where, ids)
+    s_cen = Stream(cen, cen_send, cen_recv, cen_core, where, ids)
 
     fetches[0].wait()
     own = centre_in[...]
@@ -264,7 +264,7 @@
 
     def select(e):
         da, db = ORDER[e]
-        p = member(y, z, core, da, db) // 2
+        p = lax.div(ids[da, db], 2)
         s_bnd.await_core(PLACE[db, da], 2 * p + other)
         info = bnd[2 * p, 0:32, D:WIDE].astype(jnp.float32) + bnd[2 * p + 1, 0:32, D:WIDE].astype(jnp.float32)
         both = (info[0:8] * CAP + info[8:16]) * FIELD + info[16:24]
@@ -279,34 +279,27 @@
             parts[g, p] = rows[g * 16 : (g + 1) * 16]
         for dx in (2, 1, 3):
             pltpu.make_async_remote_copy(
-                src_ref=parts.at[(x + dx) % N_GRP, p],
+                src_ref=parts.at[lax.rem(x + dx, N_GRP), p],
                 dst_ref=arrived.at[x, p],
                 send_sem=x_send.at[dx, 0],
                 recv_sem=x_recv.at[dx, 0],
-                device_id=((x + dx) % N_GRP, me),
+                device_id=(lax.rem(x + dx, N_GRP), me),
                 device_id_type=MESH,
             ).start()
         number = jnp.dot(found.astype(jnp.bfloat16), ones, preferred_element_type=jnp.float32)
         kept[...] += jnp.where(place == p, number, 0.0)
 
     kept[...] = jnp.zeros_like(kept)
-    for step in range(CHIPS + ROWS_LAG):
+    for step in range(CHIPS):
         if 0 < step < CHIPS:
             s_bnd.await_block(step)
             s_bnd.pass_on(step)
-        if step == FIRST_AT:
-            s_cen.pass_on(0, ("a", "core"))
-        if step == SECOND_AT:
-            s_cen.pass_on(0, ("b",))
-        for e in range(CHIPS):
-            if known(e) == step - ROWS_LAG:
-                select(e)
-    for g in range(N_GRP):
-        part_slots[g] = kept[g * 16 : (g + 1) * 16].astype(jnp.bfloat16)
-
+        for axis, half, at in OWN_AT:
+            if step == at:
+                s_cen.pass_on(0, (axis,), (half,))
     def across(dx, i, arriving):
-        to = (x + dx) % N_GRP
-        origin = (x - dx + N_GRP) % N_GRP if arriving else x
+        to = lax.rem(x + dx, N_GRP)
+        origin = lax.rem(x - dx + N_GRP, N_GRP) if arriving else x
         a, b = ((parts, arrived), (part_slots, arrived_slots))[i]
         return pltpu.make_async_remote_copy(
             src_ref=a.at[to],
@@ -317,14 +310,18 @@
             device_id_type=MESH,
         )
 
-    for dx in (2, 1, 3):
-        across(dx, 1, False).start()
     keeps = [
         pltpu.make_async_copy(a.at[x], b.at[x], own_sem.at[i])
         for i, (a, b) in enumerate(((parts, arrived), (part_slots, arrived_slots)))
     ]
-    for keep in keeps:
-        keep.start()
+
+    def selected():
+        for g in range(N_GRP):
+            part_slots[g] = kept[g * 16 : (g + 1) * 16].astype(jnp.bfloat16)
+        for dx in (2, 1, 3):
+            across(dx, 1, False).start()
+        for keep in keeps:
+            keep.start()
 
     def residuals():
         for dx in (1, 2, 3):
@@ -376,6 +373,16 @@
                 s_cen.await_block(e)
                 s_cen.pass_on(e)
 
+        for n, e in enumerate(sorted(range(CHIPS), key=known)):
+
+            @pl.when(i == 0 + n // 4)
+            def _(e=e):
+                select(e)
+
+        @pl.when(i == 0 + (CHIPS - 1) // 4)
+        def _():
+            selected()
+
         @pl.when(i == RESIDUALS_AT)
         def _():
             residuals()
@@ -413,7 +420,7 @@
 
     def block_of(e, side):
         da, db = offsets(e)
-        return member(y, z, (core + side) % 2, da, db)
+        return member(y, z, lax.rem(core + side, 2), da, db)
 
     def columns(block):
         return scores_out.at[:, pl.ds(pl.multiple_of(block * CEN, CEN), CEN)]

time: 66.9 us -> 65.3 us (0.976)
  Pallas kernels: 66.1 us -> 64.5 us
    pallas_call x1, Pallas kernels: 59 us -> 57.2 us  [on_device(): pl.pallas_call(gather_kernel, out_shape=(pltpu.VMEM((N_MEM, V_DEV, CEN),...]
where the time goes in v3:
time: 65.3 us; the launch traced here: 65.2 us
  Pallas kernels  64.5 us (99%)
    pallas_call x1, Pallas kernels, on_device(): pl.pallas_call(gather_kernel, out_shape=(pltpu.VMEM((N_MEM, V_DEV, CEN),...  57.2 us
    pallas_call x1, Pallas kernels, on_device(): pl.pallas_call(finish_kernel, out_shape=(jax.ShapeDtypeStruct((V_DEV, N_M...  7.39 us

profile of v3, /device:TPU:1, one launch (start us, length us, event | category | flops | bytes accessed | tf_op | source)
XLA Modules:
  0.0 65.2 jit_solution(6175813355306785028)
XLA Ops:
  0.6 57.2 %gather.1 = (bf16[32,1024,256]{2,1,0:T(8,128)(2,1)S(1)}, bf16[32,256,768]{2,1,0:T(8,128)(2,1)S(1)}, bf16[32,64,896]{2,1,0:T(8,128)(2,1)S(1)}, bf16[1024,768]{1,0...) custom-call(f32[1024,768]{1,0:T(8,128)} %vectors.1, f32[64,768]{1,0:T(8,128)} %boundary.1, ...), custom_call_target="tpu_custom_call" | custom-call | tf_op jit(solution)/shard_map/gather/pallas_call | solution.py:479
  57.8 7.4 %finish.1 = (bf16[1024,8192]{1,0:T(8,128)(2,1)}, f32[1024,768]{1,0:T(8,128)}, f32[1,1024]{1,0:T(1,128)}) custom-call(bf16[32,1024,256]{2,1,0:T(8,128)(2,1)S(1)} %get-tuple-element.9.scores, bf16[32,256,768]{2,1,0:T(8,128)(2,1)S(1)} %get-tuple-element.10.cen, bf16[32,64,896]{2,1,0:T(8,128)(2,1)S(1)} %get-tuple-element.11.bnd, ...), custom_call_target="tpu_custom_call" | custom-call | tf_op jit(solution)/shard_map/finish/pallas_call | solution.py:513

commit v4 on v3

--- a/solution.py
+++ b/solution.py
@@ -211,7 +211,6 @@
     fetches[0].wait()
     own = centre_in[...]
     cen[me] = own.astype(jnp.bfloat16)
-    pl.semaphore_wait(barrier, len(greeted))
 
     fetches[1].wait()
     fetches[2].wait()
@@ -244,6 +243,7 @@
     fetches[3].wait()
     bnd[me, :, 0:D] = rows_in[...].astype(jnp.bfloat16)
 
+    pl.semaphore_wait(barrier, len(greeted))
     s_bnd.pass_on(0)
 
     fetches[4].wait()

time: 65.3 us -> 65 us (level)
  no operation moved by 1% of the time
where the time goes in v4:
time: 65 us; the launch traced here: 64.9 us
  Pallas kernels  64.2 us (99%)
    pallas_call x1, Pallas kernels, on_device(): pl.pallas_call(gather_kernel, out_shape=(pltpu.VMEM((N_MEM, V_DEV, CEN),...  56.8 us
    pallas_call x1, Pallas kernels, on_device(): pl.pallas_call(finish_kernel, out_shape=(jax.ShapeDtypeStruct((V_DEV, N_M...  7.38 us

profile of v4, /device:TPU:1, one launch (start us, length us, event | category | flops | bytes accessed | tf_op | source)
XLA Modules:
  0.0 64.9 jit_solution(6499628788644977652)
XLA Ops:
  0.6 56.8 %gather.1 = (bf16[32,1024,256]{2,1,0:T(8,128)(2,1)S(1)}, bf16[32,256,768]{2,1,0:T(8,128)(2,1)S(1)}, bf16[32,64,896]{2,1,0:T(8,128)(2,1)S(1)}, bf16[1024,768]{1,0...) custom-call(f32[1024,768]{1,0:T(8,128)} %vectors.1, f32[64,768]{1,0:T(8,128)} %boundary.1, ...), custom_call_target="tpu_custom_call" | custom-call | tf_op jit(solution)/shard_map/gather/pallas_call | solution.py:479
  57.5 7.4 %finish.1 = (bf16[1024,8192]{1,0:T(8,128)(2,1)}, f32[1024,768]{1,0:T(8,128)}, f32[1,1024]{1,0:T(1,128)}) custom-call(bf16[32,1024,256]{2,1,0:T(8,128)(2,1)S(1)} %get-tuple-element.9.scores, bf16[32,256,768]{2,1,0:T(8,128)(2,1)S(1)} %get-tuple-element.10.cen, bf16[32,64,896]{2,1,0:T(8,128)(2,1)S(1)} %get-tuple-element.11.bnd, ...), custom_call_target="tpu_custom_call" | custom-call | tf_op jit(solution)/shard_map/finish/pallas_call | solution.py:513
